TPU v7x, 256 devices: a whole 4x4x8 slice. The times are simulated.
256 devices in a mesh: dp: 32 (over y_hi, z, core), mp: 8 (over x, y_lo).
Axes of the slice: x: 4, y: 4 (y_hi: 2, y_lo: 2; y = y_hi * 2 + y_lo), z: 8, core: 2. Of those that a mesh axis runs over, the one named last changes fastest.
Arguments:
- features: bfloat16 [32768, 4096], P('dp'), may hold values from -13 to 13
- out_grads: bfloat16 [32768, 4096], P('dp', 'mp'), may hold values from -6 to 6
- counts: int32 [32], P('dp'), may hold values from 341 to 1024, as said below
- factor_old: float32 [8, 32, 2, 512, 512], P('mp', 'dp'), may hold values from -1 to 3, as said below
- inverse_old: float32 [8, 32, 2, 512, 512], P('mp', 'dp'), may hold values from -1 to 3, as said below
- old_owner: int32 [8, 2], replicated, may hold values from 0 to 31, as said below
- new_owner: int32 [8, 2], replicated, may hold values from 0 to 31, as said below
Outputs:
- factor_new: float32 [8, 32, 512, 512], P('mp', 'dp')
- inverse_new: float32 [8, 32, 512, 512], P('mp', 'dp')
- update: float32 [4096, 4096], P('dp', 'mp')
Inputs may be any that keep to these rules, and one draw needn't show every extreme that they name: `counts`: some dp index has all 1024 rows valid. `factor_old`: Symmetric. `inverse_old`: Symmetric. `old_owner`: A dp index holds at most both blocks of one mp index; in every draw some mp index has both blocks at one dp index. `new_owner`: the two blocks of one mp index have different new owners.
All inputs are finite; a program needn't handle non-finite values.
Results may differ from a plain program's by a relative error of at most 0.0057.
Values may be sent and summed in bfloat16 or wider, within the bound.
No kernel may reach another device: no remote copies, remote signals or barrier semaphores. Data moves between devices by JAX's collectives and lax.ppermute only.
A program may use at most 128 MiB of HBM per device.

v0:
```python
import jax
import jax.numpy as jnp
from jax import lax
from jax.sharding import PartitionSpec as P

DECAY = 0.9
DAMPING = 0.01


def from_root(block, axis, owner):
    block = jnp.where(lax.axis_index(axis) == owner, block, jnp.zeros_like(block))
    return lax.psum(block, axis)


def contract_rows(first_rows, second_rows):
    return lax.dot_general(
        first_rows, second_rows, (((0,), (0,)), ((), ())), preferred_element_type=jnp.float32
    )


def refresh(stale_factor, stale_inverse, covariance, token_total):
    block_width = stale_factor.shape[0]
    factor = DECAY * stale_factor + (1.0 - DECAY) * covariance / token_total
    damped = factor + DAMPING * jnp.eye(block_width, dtype=jnp.float32)
    inner_prod = jnp.dot(damped, stale_inverse, precision=lax.Precision.HIGHEST)
    inverse = 2.0 * stale_inverse - jnp.dot(
        stale_inverse, inner_prod, precision=lax.Precision.HIGHEST
    )
    return (factor, inverse)


def local(features, out_grads, counts, factor_old, inverse_old, old_owner, new_owner):
    block_width = out_grads.shape[1]
    tok_rows = features.shape[0]
    feature_count = features.shape[1]
    column = lax.axis_index("mp")
    member = lax.axis_index("dp")
    members = lax.axis_size("dp")
    valid_rows = (jnp.arange(tok_rows, dtype=jnp.int32) < counts[0])[:, None]
    grads_kept = jnp.where(valid_rows, out_grads, jnp.zeros_like(out_grads))
    own_block = lax.dynamic_slice_in_dim(features, column * block_width, block_width, 1)
    block_kept = jnp.where(valid_rows, own_block, jnp.zeros_like(own_block))
    partials = jnp.stack(
        [contract_rows(block_kept, own_block), contract_rows(grads_kept, out_grads)]
    )
    summed, totals = lax.psum((partials, counts.astype(jnp.float32)), "dp")
    token_total = totals[0]
    stale_owner = lax.dynamic_index_in_dim(old_owner, column, 0, keepdims=False)
    fresh_owner = lax.dynamic_index_in_dim(new_owner, column, 0, keepdims=False)
    shared_slot = (stale_owner[1] == stale_owner[0]).astype(jnp.int32)
    slot_index = (jnp.zeros((), jnp.int32), shared_slot)
    held_factors = factor_old[0, 0]
    held_inverses = inverse_old[0, 0]
    blank_block = jnp.zeros((block_width, block_width), jnp.float32)
    factor_out = blank_block
    inverse_out = blank_block
    rounded = []
    for which_block in range(2):
        stale_factor = lax.dynamic_index_in_dim(
            held_factors, slot_index[which_block], 0, keepdims=False
        )
        stale_inverse = lax.dynamic_index_in_dim(
            held_inverses, slot_index[which_block], 0, keepdims=False
        )
        covariance = summed[which_block]
        factor, inverse = lax.cond(
            member == stale_owner[which_block],
            lambda: refresh(stale_factor, stale_inverse, covariance, token_total),
            lambda: (blank_block, blank_block),
        )
        both_blocks = from_root(jnp.stack([factor, inverse]), "dp", stale_owner[which_block])
        factor = both_blocks[0]
        inverse = both_blocks[1]
        rounded.append(inverse.astype(jnp.bfloat16))
        keeper = member == fresh_owner[which_block]
        factor_out = jnp.where(keeper, factor, factor_out)
        inverse_out = jnp.where(keeper, inverse, inverse_out)
    right_inverse = rounded[1]
    left_inverses = lax.all_gather(rounded[0][None], "mp", axis=0, tiled=True)
    share_rows = block_width // members
    summed_grad = lax.psum_scatter(
        contract_rows(grads_kept, features), "dp", scatter_dimension=0, tiled=True
    )
    grad_round = summed_grad.astype(jnp.bfloat16)
    stacked = grad_round.reshape(share_rows, -1, block_width)
    half_step = jnp.einsum(
        "hck,cik->hci", stacked, left_inverses, preferred_element_type=jnp.float32
    )
    half_step = half_step.reshape(share_rows, feature_count).astype(jnp.bfloat16)
    half_moved, grad_moved = (
        lax.all_to_all(half_step, "dp", split_axis=1, concat_axis=0, tiled=True),
        lax.all_to_all(grad_round, "dp", split_axis=1, concat_axis=0, tiled=True),
    )
    result_turned = contract_rows(right_inverse, half_moved)
    curvature = jnp.sum(result_turned * grad_moved.astype(jnp.float32))
    result = result_turned.T
    curvature = lax.psum(curvature, ("dp", "mp"))
    entries = float(feature_count * block_width * lax.axis_size("mp"))
    clip_scale = jnp.minimum(1.0, jnp.sqrt(entries / jnp.abs(curvature)))
    return (factor_out[None, None], inverse_out[None, None], clip_scale * result)


def solution(mesh):
    return jax.shard_map(
        local,
        mesh=mesh,
        in_specs=(
            P("dp", None),
            P("dp", "mp"),
            P("dp"),
            P("mp", "dp", None, None, None),
            P("mp", "dp", None, None, None),
            P(),
            P(),
        ),
        out_specs=(P("mp", "dp", None, None), P("mp", "dp", None, None), P("dp", "mp")),
        check_vma=False,
    )
```

profile of v0, /device:TPU:1, one launch (start us, length us, event | category | flops | bytes accessed | tf_op | source)
XLA Modules:
  0.0 956.5 jit_solution(16445997575437055482)
XLA Ops:
  7.2 0.0 all-reduce.4.cloned.1.call-start
  7.9 2.4 fusion.39
  10.3 2.4 fusion.42
  12.7 1.6 pad_maximum_fusion
  14.3 0.0 all-reduce.4.cloned.1.call-update
  14.3 0.0 all-reduce.6.cloned.1.call-start
  14.3 70.3 %psum.36 = f32[]{:T(128)} all-reduce(f32[]{:T(128)} %bitcast.12), channel_id=1, replica_groups=mesh['dp'=32,'mp'=8] {'dp'}, use_global_device_ids=true, to_apply=%region_1.2 | all-reduce | flops 1 | bytes 8 | tf_op jit(solution)/shard_map/psum | solution.py:46
  84.6 0.0 copy-done.5
  84.6 0.0 copy-done.6
  84.6 0.1 constant_dynamic-slice_fusion
  84.7 0.5 fusion.66
  87.8 201.8 %all-reduce.4.cloned.1.call-done = f32[2,512,512]{2,1,0:T(8,128)} async-done(((f32[2,512,512]{2,1,0:T(8,128)}), f32[2,512,512]{2,1,0:T(8,128)}) %all-reduce.4.cloned.1.call-update) | async-done | bytes 2097168 | tf_op jit(solution)/shard_map/psum | solution.py:46
  289.6 0.0 copy-done
  289.6 1.2 conditional.3
  289.6 0.1 stack.31
  289.7 1.1 stack.31.clone
  290.8 2.8 maximum_select_fusion.1
  293.6 1.2 conditional.2
  293.6 0.1 stack.29
  293.8 1.1 stack.29.clone
  294.9 2.8 maximum_select_fusion
  297.7 0.0 all-reduce.6.cloned.1.call-update
  297.7 0.2 reduce-scatter.2.cloned.1.call-start
  297.9 1.0 copy-done.4
  298.9 10.3 %fusion.35 = f32[512,4096]{1,0:T(8,128)} fusion(bf16[1024,4096]{1,0:T(8,128)(2,1)} %param.11, bf16[1024,512]{1,0:T(8,128)(2,1)S(1)} %copy-done.4, pred[1024]{0:T(1024)(128)(4,1)S(1)} %iota_compare_fusion.4), kind=kOutput, calls=%fused_computation.50 | convolution fusion | flops 4295491584 | bytes 17826816 | tf_op jit(solution)/shard_map/dot_general | solution.py:16
  309.2 0.0 reduce-scatter.2.cloned.1.call-update
  309.2 0.0 all-gather.2.cloned.1.call-start
  309.3 286.9 %all-reduce.6.cloned.1.call-done = (f32[2,512,512]{2,1,0:T(8,128)}, f32[2,512,512]{2,1,0:T(8,128)}) async-done(((f32[2,512,512]{2,1,0:T(8,128)}, f32[2,512,512]{2,1,0:T(8,128)}), (f32[2,512,512]{2,1,0:T(8,128)}, f32[2,512,512]{2,1,0:T(8,128)})) %all-reduce.6.cloned.1.call-update) | async-done | bytes 4194320 | tf_op jit(solution)/shard_map/psum | solution.py:12
  596.1 2.1 slice.84
  598.2 0.0 all-gather.2.cloned.1.call-update
  598.3 0.5 fusion.65
  600.1 149.4 %reduce-scatter.2.cloned.1.call-done = f32[16,4096]{1,0:T(8,128)} async-done(((f32[512,4096]{1,0:T(8,128)}), f32[16,4096]{1,0:T(8,128)}) %reduce-scatter.2.cloned.1.call-update) | async-done | bytes 262160 | tf_op jit(solution)/shard_map/reduce_scatter | solution.py:81
  749.5 1.6 copy_bitcast_fusion
  751.1 10.9 %all-to-all-start.1 = ((bf16[16,32,128]{2,0,1:T(8,128)(2,1)}), bf16[16,32,128]{2,0,1:T(8,128)(2,1)S(1)}, u32[]{:S(2)}, u32[]{:S(2)}) async-start(bf16[16,32,128]{2,0,1:T(8,128)(2,1)} %copy_bitcast_fusion), calls=%async_computation.2 | async-start | bytes 262144 | tf_op jit(solution)/shard_map/all_to_all | solution.py:92
  762.0 1.0 convert_element_type.53
  763.0 84.6 %all-gather.2.cloned.1.call-done = bf16[8,512,512]{2,1,0:T(8,128)(2,1)} async-done(((bf16[1,512,512]{2,1,0:T(8,128)(2,1)}), bf16[8,512,512]{2,1,0:T(8,128)(2,1)}) %all-gather.2.cloned.1.call-update) | async-done | bytes 4194320 | tf_op jit(solution)/shard_map/all_gather | solution.py:79
  847.6 3.5 fusion.45
  851.1 0.1 copy.28
  851.2 0.1 convert_element_type.56
  851.3 0.7 copy.29
  852.0 0.0 all-to-all-done.1
  852.0 9.2 all-to-all-start
  861.3 0.0 copy-done.2
  861.3 3.4 select_bitcast_fusion
  864.6 7.2 all-to-all-done
  871.8 0.9 fusion.58
  872.8 75.6 %psum.39 = f32[]{:T(128)} all-reduce(f32[]{:T(128)} %get-tuple-element.140), channel_id=1, replica_groups=mesh['dp'=32,'mp'=8] {'dp','mp'}, use_global_device_ids=true, to_apply=%region_10.11 | all-reduce | flops 1 | bytes 8 | tf_op jit(solution)/shard_map/psum | solution.py:97
  949.1 0.8 copy.31
  (7 shorter events, 0.0 us)
Async XLA Ops:
  7.2 282.4 %all-reduce.4.cloned.1.call-start = ((), (), s32[]{:S(2)}) async-start(), calls=%async_computation.3 | async-start | bytes 4194304 | tf_op jit(solution)/shard_map/psum | solution.py:46
  14.3 70.3 %copy-start.5 = (s32[8,2]{0,1:T(2,128)S(1)}, s32[8,2]{0,1:T(2,128)}, u32[]{:S(2)}) copy-start(s32[8,2]{0,1:T(2,128)} %param.16) | copy-start | bytes 196
  14.3 70.3 %copy-start.6 = (s32[8,2]{0,1:T(2,128)S(1)}, s32[8,2]{0,1:T(2,128)}, u32[]{:S(2)}) copy-start(s32[8,2]{0,1:T(2,128)} %param.17) | copy-start | bytes 196
  14.3 275.3 %copy-start = (f32[1,1,2,512,512]{4,3,2,1,0:T(8,128)S(1)}, f32[1,1,2,512,512]{4,3,2,1,0:T(8,128)}, u32[]{:S(2)}) copy-start(f32[1,1,2,512,512]{4,3,2,1,0:T(8,128)} %param.15) | copy-start | bytes 6291460
  14.3 581.9 %all-reduce.6.cloned.1.call-start = ((), (), s32[]{:S(2)}) async-start(), calls=%async_computation.6 | async-start | bytes 8388608 | tf_op jit(solution)/shard_map/psum | solution.py:12
  297.7 1.2 copy-start.4
  297.7 451.8 %reduce-scatter.2.cloned.1.call-start = ((), (), s32[]{:S(2)}) async-start(), calls=%async_computation.5 | async-start | bytes 8650752 | tf_op jit(solution)/shard_map/reduce_scatter | solution.py:81
  309.2 538.3 %all-gather.2.cloned.1.call-start = ((), (), s32[]{:S(2)}) async-start(), calls=%async_computation.4 | async-start | bytes 4718592 | tf_op jit(solution)/shard_map/all_gather | solution.py:79
  751.1 100.9 %all-to-all-start.1 = ((bf16[16,32,128]{2,0,1:T(8,128)(2,1)}), bf16[16,32,128]{2,0,1:T(8,128)(2,1)S(1)}, u32[]{:S(2)}, u32[]{:S(2)}) async-start(bf16[16,32,128]{2,0,1:T(8,128)(2,1)} %copy_bitcast_fusion), calls=%async_computation.2 | async-start | bytes 262144 | tf_op jit(solution)/shard_map/all_to_all | solution.py:92
  847.6 13.7 %copy-start.2 = (f32[2,512,512]{2,1,0:T(8,128)S(1)}, f32[2,512,512]{2,1,0:T(8,128)}, u32[]{:S(2)}) copy-start(f32[2,512,512]{2,1,0:T(8,128)} %get-tuple-element.133) | copy-start | bytes 6291460
  852.0 19.8 %all-to-all-start = ((bf16[16,32,128]{2,0,1:T(8,128)(2,1)}), bf16[16,32,128]{2,0,1:T(8,128)(2,1)S(1)}, u32[]{:S(2)}, u32[]{:S(2)}) async-start(bf16[16,32,128]{2,0,1:T(8,128)(2,1)} %copy.29), calls=%async_computation.1 | async-start | bytes 262144 | tf_op jit(solution)/shard_map/all_to_all | solution.py:91
Sparse Core Ops, SparseCore 0:
  14.4 275.1 all-reduce.3
  297.8 298.2 all-reduce.5
  601.2 148.2 reduce-scatter.1
  751.8 95.7 all-gather.1
where the time goes:
time: 957 us; the launch traced here: 956 us
  waiting for transfers between devices  730 us (76%)
  blocking collectives  146 us (15%)
  starting transfers between devices  20.5 us (2%)
  matrix products  19.6 us (2%)
  between operations  19.1 us (2%)
  other arithmetic  13.1 us (1%)
    psum x1, waiting for transfers between devices, from_root(): return lax.psum(block, axis)  287 us
    psum x1, waiting for transfers between devices, local(): summed, totals = lax.psum((partials, counts.astype(jnp.float32)), 'dp')  202 us
    reduce_scatter x1, waiting for transfers between devices, local(): lax.psum_scatter(contract_rows(grads_kept, features), 'dp', scatter_dimen...  149 us
    all_gather x1, waiting for transfers between devices, local(): left_inverses = lax.all_gather(rounded[0][None], 'mp', axis=0, tiled=True)  84.6 us
    psum x1, blocking collectives, local(): curvature = lax.psum(curvature, ('dp', 'mp'))  75.6 us
    psum x1, blocking collectives, local(): summed, totals = lax.psum((partials, counts.astype(jnp.float32)), 'dp')  70.3 us
  transfers between devices with their start and end apart: 6, of which 5 were waited for; matrix products, arithmetic and copies ran while one was open for 2% of the time, Pallas kernels for 0%

commit v1 on v0

--- a/solution.py
+++ b/solution.py
@@ -76,7 +76,9 @@
         factor_out = jnp.where(keeper, factor, factor_out)
         inverse_out = jnp.where(keeper, inverse, inverse_out)
     right_inverse = rounded[1]
-    left_inverses = lax.all_gather(rounded[0][None], "mp", axis=0, tiled=True)
+    left_inverses = jnp.concatenate(
+        lax.all_to_all(jnp.stack([rounded[0][None]] * lax.axis_size("mp")), "mp", 0, 0), axis=0
+    )
     share_rows = block_width // members
     summed_grad = lax.psum_scatter(
         contract_rows(grads_kept, features), "dp", scatter_dimension=0, tiled=True

time: 957 us -> 874 us (0.913)
  waiting for transfers between devices: 730 us -> 645 us
    all_gather x1 -> x0, waiting for transfers between devices: 84.6 us -> none  [local(): left_inverses = lax.all_gather(rounded[0][None], 'mp', axis=0, tiled=True)]
  transfers between devices with their start and end apart: 6 -> 6, of which waited for: 5 -> 5; matrix products, arithmetic and copies ran while one was open for 2% -> 3% of each run, Pallas kernels for 0% -> 0%
where the time goes in v1:
time: 874 us; the launch traced here: 873 us
  waiting for transfers between devices  645 us (74%)
  blocking collectives  145 us (17%)
  starting transfers between devices  20.9 us (2%)
  matrix products  19.6 us (2%)
  between operations  19.1 us (2%)
  other arithmetic  13.1 us (1%)
  local copies, waits for them, and re-layouts  9.84 us (1%)
    psum x1, waiting for transfers between devices, from_root(): return lax.psum(block, axis)  286 us
    psum x1, waiting for transfers between devices, local(): summed, totals = lax.psum((partials, counts.astype(jnp.float32)), 'dp')  202 us
    reduce_scatter x1, waiting for transfers between devices, local(): lax.psum_scatter(contract_rows(grads_kept, features), 'dp', scatter_dimen...  143 us
    psum x1, blocking collectives, local(): curvature = lax.psum(curvature, ('dp', 'mp'))  74.8 us
    psum x1, blocking collectives, local(): summed, totals = lax.psum((partials, counts.astype(jnp.float32)), 'dp')  70.3 us
  transfers between devices with their start and end apart: 6, of which 5 were waited for; matrix products, arithmetic and copies ran while one was open for 3% of the time, Pallas kernels for 0%

profile of v1, /device:TPU:1, one launch (start us, length us, event | category | flops | bytes accessed | tf_op | source)
XLA Modules:
  0.0 872.6 jit_solution(3656402731046754066)
XLA Ops:
  7.2 0.0 all-reduce.4.cloned.1.call-start
  7.9 2.4 fusion.41
  10.3 2.4 fusion.44
  12.7 1.5 pad_maximum_fusion
  14.3 0.0 all-reduce.4.cloned.1.call-update
  14.3 0.0 all-reduce.6.cloned.1.call-start
  14.3 70.3 %psum.36 = f32[]{:T(128)} all-reduce(f32[]{:T(128)} %bitcast.12), channel_id=1, replica_groups=mesh['dp'=32,'mp'=8] {'dp'}, use_global_device_ids=true, to_apply=%region_1.2 | all-reduce | flops 1 | bytes 8 | tf_op jit(solution)/shard_map/psum | solution.py:46
  84.6 0.0 copy-done.5
  84.6 0.0 copy-done.6
  84.6 0.1 constant_dynamic-slice_fusion
  84.7 0.5 fusion.74
  87.8 201.8 %all-reduce.4.cloned.1.call-done = f32[2,512,512]{2,1,0:T(8,128)} async-done(((f32[2,512,512]{2,1,0:T(8,128)}), f32[2,512,512]{2,1,0:T(8,128)}) %all-reduce.4.cloned.1.call-update) | async-done | bytes 2097168 | tf_op jit(solution)/shard_map/psum | solution.py:46
  289.6 0.0 copy-done
  289.6 1.2 conditional.3
  289.6 0.1 stack.33
  289.7 1.1 stack.33.clone
  290.8 2.8 maximum_select_fusion.1
  293.6 1.2 conditional.2
  293.6 0.1 stack.31
  293.8 1.1 stack.31.clone
  294.9 2.8 maximum_select_fusion
  297.6 0.0 all-reduce.6.cloned.1.call-update
  297.7 0.2 reduce-scatter.2.cloned.1.call-start
  297.9 1.0 copy-done.4
  298.9 10.3 %fusion.37 = f32[512,4096]{1,0:T(8,128)} fusion(bf16[1024,4096]{1,0:T(8,128)(2,1)} %param.11, bf16[1024,512]{1,0:T(8,128)(2,1)S(1)} %copy-done.4, pred[1024]{0:T(1024)(128)(4,1)S(1)} %iota_compare_fusion.4), kind=kOutput, calls=%fused_computation.52 | convolution fusion | flops 4295491584 | bytes 17826816 | tf_op jit(solution)/shard_map/dot_general | solution.py:16
  309.2 0.0 reduce-scatter.2.cloned.1.call-update
  309.2 286.5 %all-reduce.6.cloned.1.call-done = (f32[2,512,512]{2,1,0:T(8,128)}, f32[2,512,512]{2,1,0:T(8,128)}) async-done(((f32[2,512,512]{2,1,0:T(8,128)}, f32[2,512,512]{2,1,0:T(8,128)}), (f32[2,512,512]{2,1,0:T(8,128)}, f32[2,512,512]{2,1,0:T(8,128)})) %all-reduce.6.cloned.1.call-update) | async-done | bytes 4194320 | tf_op jit(solution)/shard_map/psum | solution.py:12
  595.6 1.3 fusion.62
  596.9 2.3 stack.46
  599.2 4.6 all-to-all-start
  603.8 0.5 fusion.73
  605.6 143.3 %reduce-scatter.2.cloned.1.call-done = f32[16,4096]{1,0:T(8,128)} async-done(((f32[512,4096]{1,0:T(8,128)}), f32[16,4096]{1,0:T(8,128)}) %reduce-scatter.2.cloned.1.call-update) | async-done | bytes 262160 | tf_op jit(solution)/shard_map/reduce_scatter | solution.py:83
  749.0 1.0 convert_element_type.57
  749.9 1.6 copy_bitcast_fusion
  751.5 0.0 all-to-all-done
  751.6 10.9 %all-to-all-start.2 = ((bf16[16,32,128]{2,0,1:T(8,128)(2,1)}), bf16[16,32,128]{2,0,1:T(8,128)(2,1)S(1)}, u32[]{:S(2)}, u32[]{:S(2)}) async-start(bf16[16,32,128]{2,0,1:T(8,128)(2,1)} %copy_bitcast_fusion), calls=%async_computation.3 | async-start | bytes 262144 | tf_op jit(solution)/shard_map/all_to_all | solution.py:94
  762.5 0.0 copy-start.2
  762.5 3.5 fusion.50
  766.0 0.1 copy.28
  766.1 0.1 convert_element_type.60
  766.2 0.7 copy.29
  766.9 6.1 all-to-all-done.2
  773.0 5.1 all-to-all-start.1
  778.2 3.4 select_bitcast_fusion
  781.5 7.3 all-to-all-done.1
  788.8 0.9 fusion.66
  789.8 74.8 %psum.39 = f32[]{:T(128)} all-reduce(f32[]{:T(128)} %get-tuple-element.140), channel_id=1, replica_groups=mesh['dp'=32,'mp'=8] {'dp','mp'}, use_global_device_ids=true, to_apply=%region_10.11 | all-reduce | flops 1 | bytes 8 | tf_op jit(solution)/shard_map/psum | solution.py:99
  865.3 0.8 copy.31
  (7 shorter events, 0.0 us)
Async XLA Ops:
  7.2 282.4 %all-reduce.4.cloned.1.call-start = ((), (), s32[]{:S(2)}) async-start(), calls=%async_computation.4 | async-start | bytes 4194304 | tf_op jit(solution)/shard_map/psum | solution.py:46
  14.3 70.3 %copy-start.5 = (s32[8,2]{0,1:T(2,128)S(1)}, s32[8,2]{0,1:T(2,128)}, u32[]{:S(2)}) copy-start(s32[8,2]{0,1:T(2,128)} %param.16) | copy-start | bytes 196
  14.3 70.3 %copy-start.6 = (s32[8,2]{0,1:T(2,128)S(1)}, s32[8,2]{0,1:T(2,128)}, u32[]{:S(2)}) copy-start(s32[8,2]{0,1:T(2,128)} %param.17) | copy-start | bytes 196
  14.3 275.3 %copy-start = (f32[1,1,2,512,512]{4,3,2,1,0:T(8,128)S(1)}, f32[1,1,2,512,512]{4,3,2,1,0:T(8,128)}, u32[]{:S(2)}) copy-start(f32[1,1,2,512,512]{4,3,2,1,0:T(8,128)} %param.15) | copy-start | bytes 6291460
  14.3 581.4 %all-reduce.6.cloned.1.call-start = ((), (), s32[]{:S(2)}) async-start(), calls=%async_computation.6 | async-start | bytes 8388608 | tf_op jit(solution)/shard_map/psum | solution.py:12
  297.6 1.2 copy-start.4
  297.7 451.3 %reduce-scatter.2.cloned.1.call-start = ((), (), s32[]{:S(2)}) async-start(), calls=%async_computation.5 | async-start | bytes 8650752 | tf_op jit(solution)/shard_map/reduce_scatter | solution.py:83
  599.2 152.3 %all-to-all-start = ((bf16[8,1,512,512]{3,2,1,0:T(8,128)(2,1)}), bf16[8,1,512,512]{3,2,1,0:T(8,128)(2,1)}, u32[]{:S(2)}, u32[]{:S(2)}) async-start(bf16[8,1,512,512]{3,2,1,0:T(8,128)(2,1)} %stack.46), calls=%async_computation | async-start | bytes 8388608 | tf_op jit(solution)/shard_map/all_to_all | solution.py:80
  751.6 21.5 %all-to-all-start.2 = ((bf16[16,32,128]{2,0,1:T(8,128)(2,1)}), bf16[16,32,128]{2,0,1:T(8,128)(2,1)S(1)}, u32[]{:S(2)}, u32[]{:S(2)}) async-start(bf16[16,32,128]{2,0,1:T(8,128)(2,1)} %copy_bitcast_fusion), calls=%async_computation.3 | async-start | bytes 262144 | tf_op jit(solution)/shard_map/all_to_all | solution.py:94
  762.5 15.7 %copy-start.2 = (f32[2,512,512]{2,1,0:T(8,128)S(1)}, f32[2,512,512]{2,1,0:T(8,128)}, u32[]{:S(2)}) copy-start(f32[2,512,512]{2,1,0:T(8,128)} %get-tuple-element.133) | copy-start | bytes 6291460
  773.0 15.8 %all-to-all-start.1 = ((bf16[16,32,128]{2,0,1:T(8,128)(2,1)}), bf16[16,32,128]{2,0,1:T(8,128)(2,1)S(1)}, u32[]{:S(2)}, u32[]{:S(2)}) async-start(bf16[16,32,128]{2,0,1:T(8,128)(2,1)} %copy.29), calls=%async_computation.2 | async-start | bytes 262144 | tf_op jit(solution)/shard_map/all_to_all | solution.py:93
Sparse Core Ops, SparseCore 0:
  14.4 275.1 all-reduce.3
  297.8 297.8 all-reduce.5
  600.7 148.2 reduce-scatter.1
